TPU v7x, 32 devices: a whole 2x2x4 slice. The times are simulated.
32 devices in a mesh: inst: 8 (over y, x, core), tp: 4 (over z).
Axes of the slice: x: 2, y: 2, z: 4, core: 2. Of those that a mesh axis runs over, the one named last changes fastest.
Arguments:
- source_cache: bfloat16 [8, 4, 2, 512, 1024], P('inst', 'tp'), may hold values from -6 to 6
- resident_cache: bfloat16 [8, 4, 8, 2, 512, 256], P('inst', 'tp'), may hold values from -6 to 6
- new_kv: bfloat16 [8, 12, 2, 1024], P('inst'), may hold values from -6 to 6
- queries: bfloat16 [8, 12, 4096], P('inst', None, 'tp'), may hold values from -103 to 103
- residual: bfloat16 [8, 12, 8192], P('inst'), may hold values from -1.5 to 1.5
- lengths: int32 [8, 12], P('inst'), may hold values from 1 to 512, 3072 in all within a row
- out_weight: bfloat16 [4096, 8192], P('tp'), may hold values from -0.09375 to 0.09375
Outputs:
- mixed: bfloat16 [8, 12, 8192], P('inst')
- adopted_cache: bfloat16 [8, 4, 4, 2, 512, 256], P('inst', 'tp')
All inputs are finite; a program needn't handle non-finite values.
Results may differ from a plain program's by a relative error of at most 0.0052.
Values may be sent and summed in bfloat16 or wider, within the bound.
A program may use at most 64 MiB of HBM per device.

v0:
```python
import math

import jax
import jax.numpy as jnp
from jax import lax
from jax.sharding import PartitionSpec as P

HD = 128
KVH = 8
QH = 32


def from_behind(value, axis, steps):
    count = lax.axis_size(axis)
    pairs = [(source, (source + steps) % count) for source in range(count)]
    return lax.ppermute(value, axis, pairs)


def attend(query_vector, key_cache, value_cache, incoming_key, value_fresh, seq_lengths):
    softmax_scale = 1.0 / math.sqrt(query_vector.shape[-1])
    scores = (
        jnp.einsum("bkgd,blkd->bkgl", query_vector, key_cache, preferred_element_type=jnp.float32)
        * softmax_scale
    )
    local_score = (
        jnp.einsum("heox,hex->heo", query_vector, incoming_key, preferred_element_type=jnp.float32)
        * softmax_scale
    )
    places = jnp.arange(key_cache.shape[1], dtype=jnp.int32)
    live_mask = (places[None, :] < seq_lengths[:, None])[:, None, None, :]
    scores = jnp.where(live_mask, scores, -1e30)
    top_score = jnp.maximum(jnp.max(scores, axis=-1), local_score)
    weights = jnp.where(live_mask, jnp.exp(scores - top_score[..., None]), 0.0)
    local_weight = jnp.exp(local_score - top_score)
    total = jnp.sum(weights, axis=-1) + local_weight
    probs = (weights / total[..., None]).astype(jnp.bfloat16)
    own_prob = (local_weight / total).astype(jnp.bfloat16)
    blended = jnp.einsum("bkgl,blkd->bkgd", probs, value_cache, preferred_element_type=jnp.float32)
    blended = (
        blended
        + own_prob.astype(jnp.float32)[..., None] * value_fresh.astype(jnp.float32)[:, :, None, :]
    )
    return blended.reshape(blended.shape[0], -1).astype(jnp.bfloat16)


def on_device(source_cache, resident_cache, new_kv, queries, residual, lengths, out_weight):
    tp_count = lax.axis_size("tp")
    inst_count = lax.axis_size("inst")
    tp_rank = lax.axis_index("tp")
    per_dev = queries.shape[-1] // HD
    group = QH // KVH
    kv_dev = max(1, per_dev // group)
    per_kv = per_dev // kv_dev
    req_dev = source_cache.shape[1]
    span = source_cache.shape[3]
    adopt_rows = req_dev * tp_count
    own_lengths = lengths[0]
    parted = source_cache[0].reshape(req_dev, 2, span, KVH, HD)
    if kv_dev == 1:
        parted = jnp.repeat(parted, tp_count // KVH, axis=3)
    spread_now = lax.all_to_all(
        parted.reshape(req_dev, 2, span, tp_count, kv_dev * HD),
        "tp",
        split_axis=3,
        concat_axis=0,
        tiled=True,
    )
    adopted, handed_len = from_behind(
        (spread_now, own_lengths[:adopt_rows]), "inst", inst_count // 2
    )
    adopted_flat = adopted.reshape(adopt_rows, 2, span, kv_dev * HD)
    adopted = adopted_flat.reshape(adopt_rows, 2, span, kv_dev, HD)
    resident = resident_cache[0, 0].reshape(resident_cache.shape[2], 2, span, kv_dev, HD)
    first_head = tp_rank * per_dev // group
    fresh = lax.dynamic_slice_in_dim(new_kv[0], first_head * HD, kv_dev * HD, axis=2)
    fresh = fresh.reshape(fresh.shape[0], 2, kv_dev, HD)
    query_rows = queries[0].reshape(queries.shape[1], kv_dev, per_kv, HD)
    out_adopt = attend(
        query_rows[:adopt_rows],
        adopted[:, 0],
        adopted[:, 1],
        fresh[:adopt_rows, 0],
        fresh[:adopt_rows, 1],
        handed_len,
    )
    out_res = attend(
        query_rows[adopt_rows:],
        resident[:, 0],
        resident[:, 1],
        fresh[adopt_rows:, 0],
        fresh[adopt_rows:, 1],
        own_lengths[adopt_rows:],
    )
    attn = jnp.concatenate([out_adopt, out_res], axis=0)
    value_portion = jnp.dot(attn, out_weight, preferred_element_type=jnp.float32)
    summed = lax.psum(value_portion, "tp")
    mixed = (residual[0].astype(jnp.float32) + summed).astype(jnp.bfloat16)
    return (mixed[None], adopted_flat[None, None])


def solution(mesh):
    in_specs = (
        P("inst", "tp", None, None, None),
        P("inst", "tp", None, None, None, None),
        P("inst", None, None, None),
        P("inst", None, "tp"),
        P("inst", None, None),
        P("inst", None),
        P("tp", None),
    )
    out_specs = (P("inst", None, None), P("inst", "tp", None, None, None, None))
    return jax.shard_map(
        on_device, mesh=mesh, in_specs=in_specs, out_specs=out_specs, check_vma=False
    )
```

profile of v0, /device:TPU:0, one launch (start us, length us, event | category | flops | bytes accessed | tf_op | source)
XLA Modules:
  0.0 171.1 jit_solution(7586569025606761966)
XLA Ops:
  7.2 0.0 copy-start
  7.2 2.9 %copy.17 = bf16[1,1,2,512,1024]{3,4,2,1,0:T(8,128)(2,1)S(1)} copy(bf16[1,1,2,512,1024]{4,3,2,1,0:T(8,128)(2,1)} %param.7) | data formatting | bytes 4194304 | tf_op args[0]
  10.1 1.5 copy.18
  11.6 6.4 %all-to-all-start = ((bf16[1,2,512,4,256]{2,4,1,0,3:T(8,128)(2,1)}), bf16[1,2,512,4,256]{2,4,1,0,3:T(8,128)(2,1)S(1)}, u32[]{:S(2)}, u32[]{:S(2)}) async-start(bf16[1,2,512,4,256]{2,4,1,0,3:T(8,128)(2,1)} %copy.18), calls=%async_computation | async-start | bytes 4194304 | tf_op jit(solution)/shard_map/all_to_all | solution.py:61
  18.1 0.0 all-reduce.2.cloned.1.call-start
  18.1 0.0 copy-done.3
  18.1 1.6 collective-permute-start
  19.7 0.0 copy-done
  19.7 0.1 slice_bitcast_fusion.20
  19.8 46.5 %all-to-all-done = bf16[1,2,512,4,256]{2,4,1,0,3:T(8,128)(2,1)S(1)} async-done(((bf16[1,2,512,4,256]{2,4,1,0,3:T(8,128)(2,1)}), bf16[1,2,512,4,256]{2,4,1,0,3:T(8,128)(2,1)S(1)}, u32[]{:S(2)}, u32[]{:S(2)}) %all-to-all-start) | async-done | bytes 2097184 | tf_op jit(solution)/shard_map/all_to_all | solution.py:61
  66.3 1.5 collective-permute-start.1
  67.8 0.1 iota_compare_fusion
  67.8 0.0 copy-done.2
  67.9 6.5 %copy.21 = bf16[1,1,8,2,512,256]{4,5,3,2,1,0:T(8,128)(2,1)} copy(bf16[1,1,8,2,512,256]{5,4,3,2,1,0:T(8,128)(2,1)} %param.8) | data formatting | bytes 8388608 | tf_op args[1]
  74.4 0.1 fusion.24
  74.5 2.1 %fusion.37 = (f32[8,2,4]{2,1,0:T(2,128)S(1)}, f32[8,2,4,512]{3,2,1,0:T(4,128)S(1)}) fusion(bf16[8,2,4,128]{3,2,1,0:T(4,128)(2,1)S(1)} %slice.56, bf16[8,2,512,2,128]{2,4,3,1,0:T(8,128)(2,1)} %bitcast.72, pred[8,512]{1,0:T(8,128)(4,1)S(1)} %iota_compare_fusion), kind=kOutput, calls=%fused_computation.63 | convolution fusion | flops 8486848 | bytes 2248960 | tf_op jit(solution)/shard_map/bkgd,blkd->bkgl/dot_general | solution.py:22
  76.6 0.2 fusion.10
  76.9 2.3 %fusion.6 = bf16[8,2,4,128]{3,2,1,0:T(4,128)(2,1)S(1)} fusion(bf16[8,2,512,2,128]{2,4,3,1,0:T(8,128)(2,1)} %bitcast.73, f32[8,2,4,512]{3,2,1,0:T(4,128)S(1)} %get-tuple-element.15, f32[8,2,4]{2,1,0:T(2,128)S(1)} %get-tuple-element.7, f32[8,2,4]{2,1,0:T(2,128)S(1)} %multiply_maximum_fusion, pred[8,512]{1,0:T(8,128)(4,1)S(1)} %iota_compare_fusion, ...), kind=kOutput, calls=%fused_computation.9 | convolution fusion | flops 8544256 | bytes 2257664 | tf_op jit(solution)/shard_map/bkgl,blkd->bkgd/dot_general | solution.py:38
  79.2 0.1 fusion.28
  79.3 0.0 collective-permute-done
  79.3 0.1 iota_compare_fusion.1
  79.4 33.5 %collective-permute-done.1 = bf16[4,2,512,1,256]{2,4,1,0,3:T(8,128)(2,1)} collective-permute-done((bf16[4,2,512,1,256]{2,4,1,0,3:T(8,128)(2,1)S(1)}, bf16[4,2,512,1,256]{2,4,1,0,3:T(8,128)(2,1)}, u32[]{:S(2)}, u32[]{:S(2)}) %collective-permute-start.1) | collective-permute-done | bytes 2097184 | tf_op jit(solution)/shard_map/ppermute | solution.py:16
  113.0 1.6 fusion.38
  114.5 0.2 fusion.15
  114.7 1.6 fusion.7
  116.4 8.9 %fusion.16 = f32[12,8192]{1,0:T(8,128)} fusion(bf16[1024,8192]{1,0:T(8,128)(2,1)} %param.13, bf16[8,1024]{1,0:T(8,128)(2,1)S(1)} %convert_element_type.74, bf16[4,1024]{1,0:T(4,128)(2,1)S(1)} %convert_element_type.67), kind=kOutput, calls=%fused_computation.27 | convolution fusion | flops 201375744 | bytes 17195008 | tf_op jit(solution)/shard_map/dot_general | solution.py:95
  125.3 0.0 all-reduce.2.cloned.1.call-update
  125.3 0.0 copy-start.1
  125.3 4.2 %copy.24 = bf16[1,1,4,2,512,256]{5,4,3,2,1,0:T(8,128)(2,1)} copy(bf16[1,1,4,2,512,256]{4,5,3,2,1,0:T(8,128)(2,1)} %bitcast.24) | data formatting | bytes 4194304
  129.5 33.0 %all-reduce.2.cloned.1.call-done = f32[12,8192]{1,0:T(8,128)} async-done(((f32[12,8192]{1,0:T(8,128)}), f32[12,8192]{1,0:T(8,128)}) %all-reduce.2.cloned.1.call-update) | async-done | bytes 393232 | tf_op jit(solution)/shard_map/psum | solution.py:96
  162.4 0.0 copy-done.1
  162.4 1.8 %fusion.9 = bf16[1,12,8192]{2,1,0:T(8,128)(2,1)} fusion(f32[12,8192]{1,0:T(8,128)} %all-reduce.2.cloned.1.call-done, bf16[1,12,8192]{2,1,0:T(8,128)(2,1)S(1)} %copy-done.1), kind=kLoop, calls=%fused_computation.16 | loop fusion | flops 294912 | bytes 786432 | tf_op jit(solution)/shard_map/broadcast_in_dim | solution.py:98
  (17 shorter events, 0.2 us)
Async XLA Ops:
  7.2 12.5 %copy-start = (bf16[1,12,2,1024]{3,2,1,0:T(2,128)(2,1)S(1)}, bf16[1,12,2,1024]{3,2,1,0:T(2,128)(2,1)}, u32[]{:S(2)}) copy-start(bf16[1,12,2,1024]{3,2,1,0:T(2,128)(2,1)} %param.9) | copy-start | bytes 147460
  11.6 6.5 %copy-start.3 = (s32[1,12]{1,0:T(1,128)S(1)}, s32[1,12]{1,0:T(1,128)}, u32[]{:S(2)}) copy-start(s32[1,12]{1,0:T(1,128)} %param.12) | copy-start | bytes 148
  11.6 56.2 %copy-start.2 = (bf16[1,12,1024]{2,1,0:T(8,128)(2,1)S(1)}, bf16[1,12,1024]{2,1,0:T(8,128)(2,1)}, u32[]{:S(2)}) copy-start(bf16[1,12,1024]{2,1,0:T(8,128)(2,1)} %param.10) | copy-start | bytes 73732
  11.6 54.6 %all-to-all-start = ((bf16[1,2,512,4,256]{2,4,1,0,3:T(8,128)(2,1)}), bf16[1,2,512,4,256]{2,4,1,0,3:T(8,128)(2,1)S(1)}, u32[]{:S(2)}, u32[]{:S(2)}) async-start(bf16[1,2,512,4,256]{2,4,1,0,3:T(8,128)(2,1)} %copy.18), calls=%async_computation | async-start | bytes 4194304 | tf_op jit(solution)/shard_map/all_to_all | solution.py:61
  18.1 144.4 %all-reduce.2.cloned.1.call-start = ((), (), s32[]{:S(2)}) async-start(), calls=%async_computation.1 | async-start | bytes 1048576 | tf_op jit(solution)/shard_map/psum | solution.py:96
  18.1 61.3 %collective-permute-start = (s32[4]{0:T(128)S(1)}, s32[4]{0:T(128)S(1)}, u32[]{:S(2)}, u32[]{:S(2)}) collective-permute-start(s32[4]{0:T(128)S(1)} %slice_bitcast_fusion.21), channel_id=1, source_target_pairs={{0,16},{4,20},{8,24},{12,28},{16,0},{20,4},{24,8},{28,12},{1,17},{... | collective-permute-start | bytes 56 | tf_op jit(solution)/shard_map/ppermute | solution.py:16
  66.3 46.7 %collective-permute-start.1 = (bf16[4,2,512,1,256]{2,4,1,0,3:T(8,128)(2,1)S(1)}, bf16[4,2,512,1,256]{2,4,1,0,3:T(8,128)(2,1)}, u32[]{:S(2)}, u32[]{:S(2)}) collective-permute-start(bf16[4,2,512,1,256]{2,4,1,0,3:T(8,128)(2,1)S(1)} %bitcast.74), channel_id=1, source_target_pairs={{0,16},{4,20},{8,24},{12,28},{16,0},{20,4},{24,8},{28,12},{1,17},{... | collective-permute-start | bytes 6291464 | tf_op jit(solution)/shard_map/ppermute | solution.py:16
  125.3 37.1 %copy-start.1 = (bf16[1,12,8192]{2,1,0:T(8,128)(2,1)S(1)}, bf16[1,12,8192]{2,1,0:T(8,128)(2,1)}, u32[]{:S(2)}) copy-start(bf16[1,12,8192]{2,1,0:T(8,128)(2,1)} %param.11) | copy-start | bytes 589828
Sparse Core Ops, SparseCore 0:
  125.4 36.9 all-reduce.1
where the time goes:
time: 172 us; the launch traced here: 171 us
  waiting for transfers between devices  113 us (66%)
  matrix products  16.7 us (10%)
  local copies, waits for them, and re-layouts  15.3 us (9%)
  between operations  14.1 us (8%)
  starting transfers between devices  9.56 us (6%)
  other arithmetic  2.4 us (1%)
    all_to_all x1, waiting for transfers between devices, on_device(): lax.all_to_all(parted.reshape(req_dev, 2, span, tp_count, kv_dev * HD), '...  46.5 us
    ppermute x2, waiting for transfers between devices, from_behind(): return lax.ppermute(value, axis, pairs)  33.5 us
    psum x1, waiting for transfers between devices, on_device(): summed = lax.psum(value_portion, 'tp')  33 us
    unnamed x11, local copies, waits for them, and re-layouts  13.6 us
    dot_general x1, matrix products, on_device(): jnp.dot(attn, out_weight, preferred_element_type=jnp.float32)  8.88 us
    all_to_all x1, starting transfers between devices, on_device(): lax.all_to_all(parted.reshape(req_dev, 2, span, tp_count, kv_dev * HD), '...  6.45 us
    dot_general x2, matrix products, attend(): jnp.einsum('bkgl,blkd->bkgd', probs, value_cache, preferred_element_type=...  3.92 us
    dot_general x2, matrix products, attend(): jnp.einsum('bkgd,blkd->bkgl', query_vector, key_cache, preferred_element_...  3.64 us
  transfers between devices with their start and end apart: 4, of which 3 were waited for; matrix products, arithmetic and copies ran while one was open for 9% of the time, Pallas kernels for 0%

commit v1 on v0

v1 whole, which is shorter than its diff:
```python
import functools
import math

import jax
import jax.numpy as jnp
from jax import lax
from jax.experimental import pallas as pl
from jax.experimental.pallas import tpu as pltpu
from jax.sharding import PartitionSpec as P

HD = 128
KVH = 8
QH = 32
TILE = 16
MESH = pl.DeviceIdType.MESH
BF16 = jnp.bfloat16
F32 = jnp.float32


def fold(value, rows):
    pieces = max(1, TILE // rows)
    width = value.shape[1] // pieces
    return jnp.concatenate(
        [value[:, j * width : (j + 1) * width] for j in range(pieces)], axis=0
    )


def kernel(
    dims,
    source_ref, resident_ref, newkv_ref, query_ref, resid_ref, lens_ref, weight_ref,
    mixed_ref, adopted_ref,
    cache, resident, weight, q_raw, nk_raw, rs_raw, len_raw, len_in,
    qf, nkf, resf, attn_a, attn_b, prob, own_prob,
    send_a, land_a, all_a, send_b, land_b, all_b, total_a, total_b,
    kv_send, kv_recv, len_sem, load_sem, out_sem,
    rs_send_a, rs_recv_a, ag_send_a, ag_recv_a,
    rs_send_b, rs_recv_b, ag_send_b, ag_recv_b,
):
    n_inst, n_tp, adopt, res_rows, kv_dev, per_kv, span = dims
    per_dev = kv_dev * per_kv
    group = QH // KVH
    wide = kv_dev * HD
    inst, tp = lax.axis_index("inst"), lax.axis_index("tp")
    other = lax.rem(inst + n_inst // 2, n_inst)
    scale = 1.0 / math.sqrt(HD)
    model = weight_ref.shape[1]
    share = model // n_tp

    def column(rank):
        return pl.multiple_of((rank * per_dev) // group * HD, HD)

    barrier = pltpu.get_barrier_semaphore()
    for o in range(n_tp):
        pl.semaphore_signal(barrier, inc=1, device_id=(other, lax.rem(tp + o, n_tp)), device_id_type=MESH)
        if o > 0:
            pl.semaphore_signal(barrier, inc=1, device_id=(inst, lax.rem(tp + o, n_tp)), device_id_type=MESH)
    pl.semaphore_wait(barrier, 2 * n_tp - 1)

    core = lax.rem(inst, 2)

    def handoff(which, k):
        base = (k // 2 + (n_tp // 2 if k % 2 == 0 else 0)) % n_tp
        rank = lax.rem(tp + base + core * (n_tp // 2), n_tp)
        return pltpu.make_async_remote_copy(
            src_ref=source_ref.at[0, 0, which, :, pl.ds(column(rank), wide)],
            dst_ref=cache.at[tp, which],
            send_sem=kv_send.at[which, k],
            recv_sem=kv_recv.at[which, tp],
            device_id=(other, rank),
            device_id_type=MESH,
        )

    def arrived(which, row):
        pltpu.make_async_remote_copy(
            src_ref=cache.at[row, which],
            dst_ref=cache.at[row, which],
            send_sem=kv_send.at[which, row],
            recv_sem=kv_recv.at[which, row],
            device_id=(other, row),
            device_id_type=MESH,
        ).wait_recv()

    len_copy = pltpu.make_async_remote_copy(
        src_ref=lens_ref, dst_ref=len_in, send_sem=len_sem.at[0], recv_sem=len_sem.at[1],
        device_id=(other, tp), device_id_type=MESH,
    )
    len_copy.start()
    for k in range(n_tp):
        handoff(0, k).start()

    loads = [
        pltpu.make_async_copy(src, dst, load_sem.at[j])
        for j, (src, dst) in enumerate(
            (
                (query_ref, q_raw),
                (newkv_ref, nk_raw),
                (lens_ref, len_raw),
                (resident_ref, resident),
                (resid_ref, rs_raw),
                (weight_ref, weight),
            )
        )
    ]
    for load in loads:
        load.start()
    for load in loads[:3]:
        load.wait()
    qf[...] = q_raw[0].astype(F32)
    nkf[...] = nk_raw[0, :, :, pl.ds(column(tp), wide)].astype(F32)

    head = lax.broadcasted_iota(jnp.int32, (per_dev, HD), 0)
    place = lax.broadcasted_iota(jnp.int32, (per_dev, span), 1)

    def probabilities(row, keys, length):
        q = jnp.concatenate([qf[row : row + 1, h * HD : (h + 1) * HD] for h in range(per_dev)], axis=0)
        spread = jnp.concatenate(
            [jnp.where(head // per_kv == s, q, 0.0) for s in range(kv_dev)], axis=1
        )
        score = lax.dot_general(
            spread.astype(BF16), keys, (((1,), (1,)), ((), ())), preferred_element_type=F32
        ) * scale
        own = jnp.sum(spread * nkf[row, 0:1, :], axis=1, keepdims=True) * scale
        live = place < length
        score = jnp.where(live, score, -1e30)
        top = jnp.maximum(jnp.max(score, axis=1, keepdims=True), own)
        part = jnp.where(live, jnp.exp(score - top), 0.0)
        own_part = jnp.exp(own - top)
        total = jnp.sum(part, axis=1, keepdims=True) + own_part
        return (part / total).astype(BF16), (own_part / total).astype(BF16).astype(F32)

    def blend(row, out, out_row, p, own_p, values):
        o = jnp.dot(p, values, preferred_element_type=F32) + own_p * nkf[row, 1:2, :]
        for h in range(per_dev):
            s = h // per_kv
            out[out_row : out_row + 1, h * HD : (h + 1) * HD] = o[h : h + 1, s * HD : (s + 1) * HD]

    def length_of(lens, row):
        lane = lax.broadcasted_iota(jnp.int32, lens.shape, 1)
        return jnp.sum(jnp.where(lane == row, lens, 0), axis=1, keepdims=True)

    loads[3].wait()

    for r in range(res_rows):
        row = adopt + r
        p, own_p = probabilities(row, resident[0, 0, r, 0], length_of(len_raw[...], row))
        blend(row, attn_a, r, p, own_p, resident[0, 0, r, 1])

    loads[4].wait()
    resf[...] = rs_raw[0].astype(F32)
    loads[5].wait()

    def project(attn, rows, rank, first_row, with_residual):
        pieces = max(1, TILE // rows)
        width = share // pieces
        a = attn[0:rows, :].astype(BF16)
        parts = []
        for j in range(pieces):
            at = pl.multiple_of(rank * share + j * width, HD)
            value = jnp.dot(a, weight[:, pl.ds(at, width)], preferred_element_type=F32)
            if with_residual:
                value = value + resf[first_row : first_row + rows, pl.ds(at, width)]
            parts.append(value)
        return jnp.concatenate(parts, axis=0)

    def push(src, dst, send, recv, rank, o):
        return pltpu.make_async_remote_copy(
            src_ref=src, dst_ref=dst, send_sem=send.at[o], recv_sem=recv.at[tp],
            device_id=(inst, rank), device_id_type=MESH,
        )

    def landed(buf, send, recv, rank):
        pltpu.make_async_remote_copy(
            src_ref=buf.at[rank], dst_ref=buf.at[rank], send_sem=send.at[0], recv_sem=recv.at[rank],
            device_id=(inst, rank), device_id_type=MESH,
        ).wait_recv()

    def scatter(attn, rows, first_row, buf, land, total, send, recv):
        @pl.loop(1, n_tp)
        def _(o):
            rank = lax.rem(tp + o, n_tp)
            buf[o] = project(attn, rows, rank, first_row, False).astype(BF16)
            push(buf.at[o], land.at[tp], send, recv, rank, o).start()

        total[...] = project(attn, rows, tp, first_row, True)

    def gather(buf, land, everything, total, rs_send, rs_recv, send, recv):
        for o in range(1, n_tp):
            rank = lax.rem(tp + o, n_tp)
            landed(land, rs_send, rs_recv, rank)
            total[...] += land[rank].astype(F32)
        everything[tp] = total[...].astype(BF16)
        for o in range(1, n_tp):
            push(everything.at[tp], everything.at[tp], send, recv, lax.rem(tp + o, n_tp), o).start()
        for o in range(1, n_tp):
            push(buf.at[o], land.at[tp], rs_send, rs_recv, lax.rem(tp + o, n_tp), o).wait_send()

    def finish(everything, rows, first_row, send, recv):
        for o in range(1, n_tp):
            landed(everything, send, recv, lax.rem(tp + o, n_tp))
        pieces = max(1, TILE // rows)
        width = share // pieces
        for rank in range(n_tp):
            block = everything[rank].astype(F32)
            for j in range(pieces):
                at = rank * share + j * width
                mixed_ref[first_row : first_row + rows, at : at + width] = block[j * rows : (j + 1) * rows]
        for o in range(1, n_tp):
            push(everything.at[tp], everything.at[tp], send, recv, lax.rem(tp + o, n_tp), o).wait_send()

    def keep(which, row):
        return pltpu.make_async_copy(
            cache.at[row, which], adopted_ref.at[0, 0, row, which], out_sem.at[which, row]
        )

    scatter(attn_a, res_rows, adopt, send_a, land_a, total_a, rs_send_a, rs_recv_a)
    for k in range(n_tp):
        handoff(0, k).wait_send()
        handoff(1, k).start()
    gather(send_a, land_a, all_a, total_a, rs_send_a, rs_recv_a, ag_send_a, ag_recv_a)

    len_copy.wait_recv()
    for row in range(adopt):
        arrived(0, row)
        keep(0, row).start()
        p, own_p = probabilities(row, cache[row, 0], len_in[:, row : row + 1])
        prob[row] = p.astype(F32)
        own_prob[row] = jnp.broadcast_to(own_p, (per_dev, HD))
    finish(all_a, res_rows, adopt, ag_send_a, ag_recv_a)

    for row in range(adopt):
        arrived(1, row)
        keep(1, row).start()
        blend(row, attn_b, row, prob[row].astype(BF16), own_prob[row][:, 0:1], cache[row, 1])
    scatter(attn_b, adopt, 0, send_b, land_b, total_b, rs_send_b, rs_recv_b)
    gather(send_b, land_b, all_b, total_b, rs_send_b, rs_recv_b, ag_send_b, ag_recv_b)
    finish(all_b, adopt, 0, ag_send_b, ag_recv_b)

    len_copy.wait_send()
    for k in range(n_tp):
        handoff(1, k).wait_send()
    for which in range(2):
        for row in range(adopt):
            keep(which, row).wait()


def on_device(n_inst, n_tp, source_cache, resident_cache, new_kv, queries, residual, lengths, out_weight):
    rows = queries.shape[1]
    span = source_cache.shape[3]
    adopt = source_cache.shape[1] * n_tp
    res_rows = resident_cache.shape[2]
    per_dev = queries.shape[2] // HD
    group = QH // KVH
    kv_dev = max(1, per_dev // group)
    per_kv = per_dev // kv_dev
    wide = kv_dev * HD
    depth, model = out_weight.shape
    share = model // n_tp
    fold_a = (TILE if res_rows < TILE else res_rows, share // max(1, TILE // res_rows))
    fold_b = (TILE if adopt < TILE else adopt, share // max(1, TILE // adopt))
    dims = (n_inst, n_tp, adopt, res_rows, kv_dev, per_kv, span)
    dma = pltpu.SemaphoreType.DMA
    any_spec = pl.BlockSpec(memory_space=pl.ANY)
    mixed, adopted = pl.pallas_call(
        functools.partial(kernel, dims),
        out_shape=(
            jax.ShapeDtypeStruct((rows, model), F32),
            jax.ShapeDtypeStruct((1, 1, adopt, 2, span, wide), BF16),
        ),
        in_specs=[any_spec] * 7,
        out_specs=(pl.BlockSpec(memory_space=pltpu.VMEM), any_spec),
        scratch_shapes=[
            pltpu.VMEM((adopt, 2, span, wide), BF16),
            pltpu.VMEM(resident_cache.shape, BF16),
            pltpu.VMEM(out_weight.shape, BF16),
            pltpu.VMEM(queries.shape, BF16),
            pltpu.VMEM(new_kv.shape, BF16),
            pltpu.VMEM(residual.shape, BF16),
            pltpu.VMEM(lengths.shape, jnp.int32),
            pltpu.VMEM(lengths.shape, jnp.int32),
            pltpu.VMEM(queries.shape[1:], F32),
            pltpu.VMEM((rows, 2, wide), F32),
            pltpu.VMEM((rows, model), F32),
            pltpu.VMEM((res_rows, depth), F32),
            pltpu.VMEM((adopt, depth), F32),
            pltpu.VMEM((adopt, per_dev, span), F32),
            pltpu.VMEM((adopt, per_dev, HD), F32),
            pltpu.VMEM((n_tp,) + fold_a, BF16),
            pltpu.VMEM((n_tp,) + fold_a, BF16),
            pltpu.VMEM((n_tp,) + fold_a, BF16),
            pltpu.VMEM((n_tp,) + fold_b, BF16),
            pltpu.VMEM((n_tp,) + fold_b, BF16),
            pltpu.VMEM((n_tp,) + fold_b, BF16),
            pltpu.VMEM(fold_a, F32),
            pltpu.VMEM(fold_b, F32),
            dma((2, n_tp)),
            dma((2, n_tp)),
            dma((2,)),
            dma((6,)),
            dma((2, adopt)),
        ]
        + [dma((n_tp,))] * 8,
        compiler_params=pltpu.CompilerParams(
            collective_id=0, has_side_effects=True, vmem_limit_bytes=48 * 1024 * 1024
        ),
        cost_estimate=pl.CostEstimate(
            flops=2 * rows * depth * model, bytes_accessed=2 * depth * model, transcendentals=0
        ),
        name="handoff_attention",
    )(source_cache, resident_cache, new_kv, queries, residual, lengths, out_weight)
    return (mixed.astype(BF16)[None], adopted)


def solution(mesh):
    in_specs = (
        P("inst", "tp", None, None, None),
        P("inst", "tp", None, None, None, None),
        P("inst", None, None, None),
        P("inst", None, "tp"),
        P("inst", None, None),
        P("inst", None),
        P("tp", None),
    )
    out_specs = (P("inst", None, None), P("inst", "tp", None, None, None, None))
    return jax.shard_map(
        functools.partial(on_device, mesh.shape["inst"], mesh.shape["tp"]),
        mesh=mesh, in_specs=in_specs, out_specs=out_specs, check_vma=False,
    )
```

time: 172 us -> 75.6 us (0.44)
  waiting for transfers between devices: 113 us -> 0 us
  Pallas kernels: 0 us -> 67.8 us
  matrix products: 16.7 us -> 0 us
  between operations: 14.1 us -> 0.65 us
  starting transfers between devices: 9.56 us -> 0 us
  local copies, waits for them, and re-layouts: 15.3 us -> 6.06 us
    pallas_call x0 -> x1, Pallas kernels: none -> 67.8 us  [on_device(): pl.pallas_call(functools.partial(kernel, dims), out_shape=(jax.ShapeDtype...]
    all_to_all x1 -> x0, waiting for transfers between devices: 46.5 us -> none  [on_device(): lax.all_to_all(parted.reshape(req_dev, 2, span, tp_count, kv_dev * HD), '...]
    ppermute x2 -> x0, waiting for transfers between devices: 33.5 us -> none  [from_behind(): return lax.ppermute(value, axis, pairs)]
    psum x1 -> x0, waiting for transfers between devices: 33 us -> none  [on_device(): summed = lax.psum(value_portion, 'tp')]
    dot_general x7 -> x0, matrix products: 16.7 us -> none  [the longest x1 8.88 us: on_device(): jnp.dot(attn, out_weight, preferred_element_type=jnp.float32)]
    unnamed x11, local copies, waits for them, and re-layouts: 13.6 us -> 6.06 us
    all_to_all x1 -> x0, starting transfers between devices: 6.45 us -> none  [on_device(): lax.all_to_all(parted.reshape(req_dev, 2, span, tp_count, kv_dev * HD), '...]
    ppermute x2 -> x0, starting transfers between devices: 3.1 us -> none  [from_behind(): return lax.ppermute(value, axis, pairs)]
  transfers between devices with their start and end apart: 4 -> 0, of which waited for: 3 -> 0; matrix products, arithmetic and copies ran while one was open for 9% -> 0% of each run, Pallas kernels for 0% -> 0%
where the time goes in v1:
time: 75.6 us; the launch traced here: 75.2 us
  Pallas kernels  67.8 us (90%)
  local copies, waits for them, and re-layouts  6.06 us (8%)
    pallas_call x1, Pallas kernels, on_device(): pl.pallas_call(functools.partial(kernel, dims), out_shape=(jax.ShapeDtype...  67.8 us
    unnamed x11, local copies, waits for them, and re-layouts  6.06 us

profile of v1, /device:TPU:0, one launch (start us, length us, event | category | flops | bytes accessed | tf_op | source)
XLA Modules:
  0.0 75.2 jit_solution(16777683282749027599)
XLA Ops:
  0.6 0.0 copy-start
  0.6 1.6 %copy-done = bf16[1,1,2,512,1024]{4,3,2,1,0:T(8,128)(2,1)S(1)} copy-done((bf16[1,1,2,512,1024]{4,3,2,1,0:T(8,128)(2,1)S(1)}, bf16[1,1,2,512,1024]{4,3,2,1,0:T(8,128)(2,1)}, u32[]{:S(2)}) %copy-start) | copy-done | bytes 2097176
  2.2 0.0 copy-start.1
  2.2 0.9 %copy-done.1 = bf16[1,12,8192]{2,1,0:T(8,128)(2,1)S(1)} copy-done((bf16[1,12,8192]{2,1,0:T(8,128)(2,1)S(1)}, bf16[1,12,8192]{2,1,0:T(8,128)(2,1)}, u32[]{:S(2)}) %copy-start.1) | copy-done | bytes 196632
  3.2 0.0 copy-start.2
  3.2 0.8 %copy-done.2 = bf16[1,12,2,1024]{3,2,1,0:T(2,128)(2,1)S(1)} copy-done((bf16[1,12,2,1024]{3,2,1,0:T(2,128)(2,1)S(1)}, bf16[1,12,2,1024]{3,2,1,0:T(2,128)(2,1)}, u32[]{:S(2)}) %copy-start.2) | copy-done | bytes 49176
  4.0 0.0 copy-start.3
  4.0 0.8 %copy-done.3 = bf16[1,12,1024]{2,1,0:T(8,128)(2,1)S(1)} copy-done((bf16[1,12,1024]{2,1,0:T(8,128)(2,1)S(1)}, bf16[1,12,1024]{2,1,0:T(8,128)(2,1)}, u32[]{:S(2)}) %copy-start.3) | copy-done | bytes 24600
  4.7 0.0 copy-start.4
  4.7 0.7 copy-done.4
  5.4 67.8 %handoff_attention.1 = (f32[12,8192]{1,0:T(8,128)S(1)}, bf16[1,1,4,2,512,256]{5,4,3,2,1,0:T(8,128)(2,1)S(1)}) custom-call(bf16[1,1,2,512,1024]{4,3,2,1,0:T(8,128)(2,1)S(1)} %copy-done, bf16[1,1,8,2,512,256]{5,4,3,2,1,0:T(8,128)(2,1)} %resident_ref.1, bf16[1,12,2,1024]{3,2,1,0:T(2,128)(2,1)S(1)} %copy-done.2, bf16[1,12,1024]{2,1,0:T(8,128)(2,1)S(1)} %copy-done.3, ...), custom_call_target="tpu_custom_call" | custom-call | flops 201326592 | bytes 16777216 | tf_op jit(solution)/shard_map/handoff_attention/pallas_call | solution.py:263
  73.2 0.7 convert_bitcast_fusion
  73.9 1.3 %copy.10 = bf16[1,1,4,2,512,256]{5,4,3,2,1,0:T(8,128)(2,1)} copy(bf16[1,1,4,2,512,256]{5,4,3,2,1,0:T(8,128)(2,1)S(1)} %get-tuple-element.9) | data formatting | bytes 4194304
Async XLA Ops:
  0.6 1.6 %copy-start = (bf16[1,1,2,512,1024]{4,3,2,1,0:T(8,128)(2,1)S(1)}, bf16[1,1,2,512,1024]{4,3,2,1,0:T(8,128)(2,1)}, u32[]{:S(2)}) copy-start(bf16[1,1,2,512,1024]{4,3,2,1,0:T(8,128)(2,1)} %source_ref.1) | copy-start | bytes 6291460
  2.2 0.9 %copy-start.1 = (bf16[1,12,8192]{2,1,0:T(8,128)(2,1)S(1)}, bf16[1,12,8192]{2,1,0:T(8,128)(2,1)}, u32[]{:S(2)}) copy-start(bf16[1,12,8192]{2,1,0:T(8,128)(2,1)} %resid_ref.1) | copy-start | bytes 589828
  3.2 0.8 %copy-start.2 = (bf16[1,12,2,1024]{3,2,1,0:T(2,128)(2,1)S(1)}, bf16[1,12,2,1024]{3,2,1,0:T(2,128)(2,1)}, u32[]{:S(2)}) copy-start(bf16[1,12,2,1024]{3,2,1,0:T(2,128)(2,1)} %newkv_ref.1) | copy-start | bytes 147460
  4.0 0.8 %copy-start.3 = (bf16[1,12,1024]{2,1,0:T(8,128)(2,1)S(1)}, bf16[1,12,1024]{2,1,0:T(8,128)(2,1)}, u32[]{:S(2)}) copy-start(bf16[1,12,1024]{2,1,0:T(8,128)(2,1)} %query_ref.1) | copy-start | bytes 73732
  4.7 0.7 copy-start.4

commit v2 on v1

v2 whole, which is shorter than its diff:
```python
import functools
import math

import jax
import jax.numpy as jnp
from jax import lax
from jax.experimental import pallas as pl
from jax.experimental.pallas import tpu as pltpu
from jax.sharding import PartitionSpec as P

HD = 128
KVH = 8
QH = 32
TILE = 16
MESH = pl.DeviceIdType.MESH
BF16 = jnp.bfloat16
F32 = jnp.float32


def pieces_of(rows):
    return TILE // math.gcd(rows, TILE)


def kernel(
    dims,
    source_ref, resident_ref, newkv_ref, query_ref, resid_ref, lens_ref, weight_ref,
    mixed_ref, adopted_ref,
    source, resident, weight, q_raw, nk_raw, rs_raw, len_raw,
    qf, q_rows, q_in, nkf, nk_out, nk_in, resf, o_out, o_in, attn,
    part_out, part_in, final, total, mixed,
    kv_send, kv_recv, load_sem, q_send, q_recv, nk_sem, o_send, o_recv,
    rs_send, rs_recv, ag_send, ag_recv,
):
    n_inst, n_tp, adopt, res_rows, kv_dev, per_kv, span = dims
    rows = adopt + res_rows
    per_dev = kv_dev * per_kv
    group = QH // KVH
    wide = kv_dev * HD
    inst, tp = lax.axis_index("inst"), lax.axis_index("tp")
    other = lax.rem(inst + n_inst // 2, n_inst)
    scale = 1.0 / math.sqrt(HD)
    model = weight_ref.shape[1]
    share = model // n_tp
    pieces = pieces_of(rows)
    width = share // pieces

    def column(rank):
        return rank * per_dev // group * HD

    def my_columns(rank):
        return pl.ds(pl.multiple_of(column(rank), HD), wide)

    barrier = pltpu.get_barrier_semaphore()
    for o in range(n_tp):
        pl.semaphore_signal(barrier, inc=1, device_id=(other, lax.rem(tp + o, n_tp)), device_id_type=MESH)
        if o > 0:
            pl.semaphore_signal(barrier, inc=1, device_id=(inst, lax.rem(tp + o, n_tp)), device_id_type=MESH)
    loads = [
        pltpu.make_async_copy(src, dst, load_sem.at[j])
        for j, (src, dst) in enumerate(
            (
                (query_ref, q_raw),
                (newkv_ref, nk_raw),
                (lens_ref, len_raw),
                (resident_ref, resident),
                (source_ref, source),
                (resid_ref, rs_raw),
                (weight_ref, weight),
            )
        )
    ]
    for load in loads[:3]:
        load.start()
    pl.semaphore_wait(barrier, 2 * n_tp - 1)

    core = lax.rem(inst, 2)

    def handoff(which, k):
        base = (k // 2 + (n_tp // 2 if k % 2 == 0 else 0)) % n_tp
        rank = lax.rem(tp + base + core * (n_tp // 2), n_tp)
        return pltpu.make_async_remote_copy(
            src_ref=source_ref.at[0, 0, which, :, my_columns(rank)],
            dst_ref=adopted_ref.at[0, 0, tp, which],
            send_sem=kv_send.at[which, k],
            recv_sem=kv_recv.at[which, tp],
            device_id=(other, rank),
            device_id_type=MESH,
        )

    def send(src, dst, send_sem, recv_sem, device):
        return pltpu.make_async_remote_copy(
            src_ref=src, dst_ref=dst, send_sem=send_sem, recv_sem=recv_sem,
            device_id=device, device_id_type=MESH,
        )

    for k in range(n_tp):
        handoff(0, k).start()
    for load in loads[3:]:
        load.start()
    for load in loads[:3]:
        load.wait()

    def rows_to_heads(first, last):
        for row in range(first, last):
            q_rows[row] = jnp.concatenate(
                [qf[row : row + 1, h * HD : (h + 1) * HD] for h in range(per_dev)], axis=0
            )

    qf[...] = q_raw[0].astype(F32)
    nk_out[...] = nk_raw[0, tp].astype(F32)
    rows_to_heads(0, adopt)
    q_sends = [
        send(q_rows.at[r], q_in.at[tp], q_send.at[r], q_recv.at[tp], (other, r)) for r in range(adopt)
    ]
    nk_send = send(nk_out, nk_in, nk_sem.at[0], nk_sem.at[1], (other, tp))
    for copy in q_sends:
        copy.start()
    nk_send.start()
    rows_to_heads(adopt, rows)
    nkf[...] = nk_raw[0, :, :, my_columns(tp)].astype(F32)

    head = lax.broadcasted_iota(jnp.int32, (per_dev, HD), 0)
    place = lax.broadcasted_iota(jnp.int32, (per_dev, span), 1)

    def attention(q, keys, values, own_key, own_value, length):
        spread = jnp.concatenate(
            [jnp.where(head // per_kv == s, q, 0.0) for s in range(kv_dev)], axis=1
        )
        score = lax.dot_general(
            spread.astype(BF16), keys, (((1,), (1,)), ((), ())), preferred_element_type=F32
        ) * scale
        own = jnp.sum(spread * own_key, axis=1, keepdims=True) * scale
        live = place < length
        score = jnp.where(live, score, -1e30)
        top = jnp.maximum(jnp.max(score, axis=1, keepdims=True), own)
        part = jnp.where(live, jnp.exp(score - top), 0.0)
        own_part = jnp.exp(own - top)
        whole = jnp.sum(part, axis=1, keepdims=True) + own_part
        p = (part / whole).astype(BF16)
        own_p = (own_part / whole).astype(BF16).astype(F32)
        o = jnp.dot(p, values, preferred_element_type=F32) + own_p * own_value
        result = o[:, 0:HD]
        for s in range(1, kv_dev):
            result = jnp.where(head // per_kv == s, o[:, s * HD : (s + 1) * HD], result)
        return result

    def place_row(row, heads):
        for h in range(per_dev):
            attn[row : row + 1, h * HD : (h + 1) * HD] = heads[h : h + 1, :]

    lens = len_raw[...]
    lane = lax.broadcasted_iota(jnp.int32, lens.shape, 1)
    handed = jnp.sum(jnp.where(lane == tp, lens, 0), axis=1, keepdims=True)

    def serve(row):
        r = row - adopt
        place_row(
            row,
            attention(
                q_rows[row], resident[0, 0, r, 0], resident[0, 0, r, 1],
                nkf[row, 0:1, :], nkf[row, 1:2, :], lens[:, row : row + 1],
            ),
        )

    loads[3].wait()
    for row in range(adopt, adopt + res_rows // 2):
        serve(row)

    loads[4].wait()
    nk_send.wait_recv()
    for rank in range(n_tp):
        send(q_rows.at[rank], q_in.at[rank], q_send.at[rank], q_recv.at[rank], (other, rank)).wait_recv()
    o_sends = []
    for rank in range(n_tp):
        at = column(rank)
        o_out[rank] = attention(
            q_in[rank], source[0, 0, 0, :, at : at + wide], source[0, 0, 1, :, at : at + wide],
            nk_in[0:1, at : at + wide], nk_in[1:2, at : at + wide], handed,
        )
        copy = send(o_out.at[rank], o_in.at[tp], o_send.at[rank], o_recv.at[tp], (other, rank))
        copy.start()
        o_sends.append(copy)
    for k in range(n_tp // 2):
        handoff(1, k).start()

    for row in range(adopt + res_rows // 2, rows):
        serve(row)
    loads[5].wait()
    resf[...] = rs_raw[0].astype(F32)
    for row in range(adopt):
        send(o_out.at[row], o_in.at[row], o_send.at[row], o_recv.at[row], (other, row)).wait_recv()
        place_row(row, o_in[row])
    loads[6].wait()

    def project(rank, with_residual):
        a = attn[...].astype(BF16)
        parts = []
        for j in range(pieces):
            at = pl.multiple_of(rank * share + j * width, HD)
            value = jnp.dot(a, weight[:, pl.ds(at, width)], preferred_element_type=F32)
            if with_residual:
                value = value + resf[:, pl.ds(at, width)]
            parts.append(value)
        return jnp.concatenate(parts, axis=0)

    @pl.loop(1, n_tp)
    def _(o):
        rank = lax.rem(tp + o, n_tp)
        part_out[o] = project(rank, False).astype(BF16)
        send(part_out.at[o], part_in.at[tp], rs_send.at[o], rs_recv.at[tp], (inst, rank)).start()

    for k in range(n_tp // 2, n_tp):
        handoff(1, k).start()
    total[...] = project(tp, True)
    for o in range(1, n_tp):
        rank = lax.rem(tp + o, n_tp)
        send(part_out.at[o], part_in.at[rank], rs_send.at[o], rs_recv.at[rank], (inst, rank)).wait_recv()
        total[...] += part_in[rank].astype(F32)
    final[tp] = total[...].astype(BF16)

    def give(o):
        rank = lax.rem(tp + o, n_tp)
        return send(final.at[tp], final.at[tp], ag_send.at[o], ag_recv.at[tp], (inst, rank))

    for o in range(1, n_tp):
        give(o).start()
    for o in range(1, n_tp):
        rank = lax.rem(tp + o, n_tp)
        send(final.at[rank], final.at[rank], ag_send.at[o], ag_recv.at[rank], (inst, rank)).wait_recv()
    for rank in range(n_tp):
        block = final[rank].astype(F32)
        for j in range(pieces):
            at = rank * share + j * width
            mixed[:, at : at + width] = block[j * rows : (j + 1) * rows].astype(BF16)
    mixed_copy = pltpu.make_async_copy(mixed, mixed_ref, load_sem.at[7])
    mixed_copy.start()

    mixed_copy.wait()
    for copy in q_sends:
        copy.wait_send()
    nk_send.wait_send()
    for copy in o_sends:
        copy.wait_send()
    for o in range(1, n_tp):
        rank = lax.rem(tp + o, n_tp)
        send(part_out.at[o], part_in.at[tp], rs_send.at[o], rs_recv.at[tp], (inst, rank)).wait_send()
        give(o).wait_send()
    for which in range(2):
        for k in range(n_tp):
            handoff(which, k).wait_send()
            there = adopted_ref.at[0, 0, k, which]
            send(there, there, kv_send.at[which, k], kv_recv.at[which, k], (other, k)).wait_recv()


def on_device(n_inst, n_tp, source_cache, resident_cache, new_kv, queries, residual, lengths, out_weight):
    rows = queries.shape[1]
    span = source_cache.shape[3]
    adopt = source_cache.shape[1] * n_tp
    res_rows = resident_cache.shape[2]
    per_dev = queries.shape[2] // HD
    group = QH // KVH
    kv_dev = max(1, per_dev // group)
    per_kv = per_dev // kv_dev
    wide = kv_dev * HD
    depth, model = out_weight.shape
    pieces = pieces_of(rows)
    stack = (rows * pieces, model // n_tp // pieces)
    dims = (n_inst, n_tp, adopt, res_rows, kv_dev, per_kv, span)
    dma = pltpu.SemaphoreType.DMA
    any_spec = pl.BlockSpec(memory_space=pl.ANY)
    mixed, adopted = pl.pallas_call(
        functools.partial(kernel, dims),
        out_shape=(
            jax.ShapeDtypeStruct((rows, model), BF16),
            jax.ShapeDtypeStruct((1, 1, adopt, 2, span, wide), BF16),
        ),
        in_specs=[pl.BlockSpec(memory_space=pltpu.HBM)] * 7,
        out_specs=(any_spec, any_spec),
        scratch_shapes=[
            pltpu.VMEM(source_cache.shape, BF16),
            pltpu.VMEM(resident_cache.shape, BF16),
            pltpu.VMEM(out_weight.shape, BF16),
            pltpu.VMEM(queries.shape, BF16),
            pltpu.VMEM(new_kv.shape, BF16),
            pltpu.VMEM(residual.shape, BF16),
            pltpu.VMEM(lengths.shape, jnp.int32),
            pltpu.VMEM(queries.shape[1:], F32),
            pltpu.VMEM((rows, per_dev, HD), F32),
            pltpu.VMEM((n_tp, per_dev, HD), F32),
            pltpu.VMEM((rows, 2, wide), F32),
            pltpu.VMEM(new_kv.shape[2:], F32),
            pltpu.VMEM(new_kv.shape[2:], F32),
            pltpu.VMEM((rows, model), F32),
            pltpu.VMEM((n_tp, per_dev, HD), F32),
            pltpu.VMEM((adopt, per_dev, HD), F32),
            pltpu.VMEM((rows, depth), F32),
            pltpu.VMEM((n_tp,) + stack, BF16),
            pltpu.VMEM((n_tp,) + stack, BF16),
            pltpu.VMEM((n_tp,) + stack, BF16),
            pltpu.VMEM(stack, F32),
            pltpu.VMEM((rows, model), BF16),
            dma((2, n_tp)),
            dma((2, n_tp)),
            dma((8,)),
            dma((adopt,)),
            dma((n_tp,)),
            dma((2,)),
            dma((n_tp,)),
            dma((adopt,)),
        ]
        + [dma((n_tp,))] * 4,
        compiler_params=pltpu.CompilerParams(
            collective_id=0, has_side_effects=True, vmem_limit_bytes=60 * 1024 * 1024
        ),
        cost_estimate=pl.CostEstimate(
            flops=2 * rows * depth * model, bytes_accessed=2 * depth * model, transcendentals=0
        ),
        name="handoff_attention",
    )(source_cache, resident_cache, new_kv, queries, residual, lengths, out_weight)
    return (mixed[None], adopted)


def solution(mesh):
    in_specs = (
        P("inst", "tp", None, None, None),
        P("inst", "tp", None, None, None, None),
        P("inst", None, None, None),
        P("inst", None, "tp"),
        P("inst", None, None),
        P("inst", None),
        P("tp", None),
    )
    out_specs = (P("inst", None, None), P("inst", "tp", None, None, None, None))
    return jax.shard_map(
        functools.partial(on_device, mesh.shape["inst"], mesh.shape["tp"]),
        mesh=mesh, in_specs=in_specs, out_specs=out_specs, check_vma=False,
    )
```

time: 75.6 us -> 71.3 us (0.943)
  Pallas kernels: 67.8 us -> 65.8 us
  local copies, waits for them, and re-layouts: 6.06 us -> 4.71 us
    pallas_call x1, Pallas kernels: 67.8 us -> 65.8 us  [on_device(): pl.pallas_call(functools.partial(kernel, dims), out_shape=(jax.ShapeDtype...]
    unnamed x11 -> x2, local copies, waits for them, and re-layouts: 6.06 us -> 4.71 us
where the time goes in v2:
time: 71.3 us; the launch traced here: 71.1 us
  Pallas kernels  65.8 us (92%)
  local copies, waits for them, and re-layouts  4.71 us (7%)
    pallas_call x1, Pallas kernels, on_device(): pl.pallas_call(functools.partial(kernel, dims), out_shape=(jax.ShapeDtype...  65.8 us
    unnamed x2, local copies, waits for them, and re-layouts  4.71 us

profile of v2, /device:TPU:0, one launch (start us, length us, event | category | flops | bytes accessed | tf_op | source)
XLA Modules:
  0.0 71.1 jit_solution(16412229950454372911)
XLA Ops:
  0.6 65.8 %handoff_attention.1 = (bf16[12,8192]{1,0:T(8,128)(2,1)}, bf16[1,1,4,2,512,256]{5,4,3,2,1,0:T(8,128)(2,1)}) custom-call(bf16[1,1,2,512,1024]{4,3,2,1,0:T(8,128)(2,1)} %source_ref.1, bf16[1,1,8,2,512,256]{5,4,3,2,1,0:T(8,128)(2,1)} %resident_ref.1, bf16[1,12,2,1024]{3,2,1,0:T(2,128)(2,1)} %newkv_ref.1, bf16[1,12,1024]{2,1,0:T(8,128)(2,1)} %query_ref.1, ...), custom_call_target="tpu_custom_call" | custom-call | flops 201326592 | bytes 16777216 | tf_op jit(solution)/shard_map/handoff_attention/pallas_call | solution.py:271
  66.4 1.7 %copy.11 = bf16[1,12,8192]{2,1,0:T(8,128)(2,1)} copy(bf16[1,12,8192]{2,1,0:T(8,128)(2,1)} %bitcast.1) | data formatting | bytes 393216
  68.1 3.0 %copy.12 = bf16[1,1,4,2,512,256]{5,4,3,2,1,0:T(8,128)(2,1)} copy(bf16[1,1,4,2,512,256]{5,4,3,2,1,0:T(8,128)(2,1)} %get-tuple-element.9) | data formatting | bytes 4194304

commit v3 on v2

--- a/solution.py
+++ b/solution.py
@@ -75,17 +75,26 @@
 
     core = lax.rem(inst, 2)
 
-    def handoff(which, k):
+    half = span // 2
+
+    def handoff(j):
+        phase, k = j // n_tp, j % n_tp
+        which, piece = phase // 2, phase % 2
         base = (k // 2 + (n_tp // 2 if k % 2 == 0 else 0)) % n_tp
         rank = lax.rem(tp + base + core * (n_tp // 2), n_tp)
+        rows_of = pl.ds(piece * half, half)
         return pltpu.make_async_remote_copy(
-            src_ref=source_ref.at[0, 0, which, :, my_columns(rank)],
-            dst_ref=adopted_ref.at[0, 0, tp, which],
-            send_sem=kv_send.at[which, k],
-            recv_sem=kv_recv.at[which, tp],
+            src_ref=source_ref.at[0, 0, which, rows_of, my_columns(rank)],
+            dst_ref=adopted_ref.at[0, 0, tp, which, rows_of],
+            send_sem=kv_send.at[phase, k],
+            recv_sem=kv_recv.at[phase, tp],
             device_id=(other, rank),
             device_id_type=MESH,
         )
+
+    def start_handoff(first, last):
+        for j in range(first * n_tp // 4, last * n_tp // 4):
+            handoff(j).start()
 
     def send(src, dst, send_sem, recv_sem, device):
         return pltpu.make_async_remote_copy(
@@ -93,8 +102,7 @@
             device_id=device, device_id_type=MESH,
         )
 
-    for k in range(n_tp):
-        handoff(0, k).start()
+    start_handoff(0, 2)
     for load in loads[3:]:
         load.start()
     for load in loads[:3]:
@@ -116,6 +124,7 @@
     for copy in q_sends:
         copy.start()
     nk_send.start()
+    start_handoff(2, 6)
     rows_to_heads(adopt, rows)
     nkf[...] = nk_raw[0, :, :, my_columns(tp)].astype(F32)
 
@@ -180,8 +189,7 @@
         copy = send(o_out.at[rank], o_in.at[tp], o_send.at[rank], o_recv.at[tp], (other, rank))
         copy.start()
         o_sends.append(copy)
-    for k in range(n_tp // 2):
-        handoff(1, k).start()
+    start_handoff(6, 10)
 
     for row in range(adopt + res_rows // 2, rows):
         serve(row)
@@ -209,8 +217,7 @@
         part_out[o] = project(rank, False).astype(BF16)
         send(part_out.at[o], part_in.at[tp], rs_send.at[o], rs_recv.at[tp], (inst, rank)).start()
 
-    for k in range(n_tp // 2, n_tp):
-        handoff(1, k).start()
+    start_handoff(10, 12)
     total[...] = project(tp, True)
     for o in range(1, n_tp):
         rank = lax.rem(tp + o, n_tp)
@@ -224,6 +231,7 @@
 
     for o in range(1, n_tp):
         give(o).start()
+    start_handoff(12, 16)
     for o in range(1, n_tp):
         rank = lax.rem(tp + o, n_tp)
         send(final.at[rank], final.at[rank], ag_send.at[o], ag_recv.at[rank], (inst, rank)).wait_recv()
@@ -245,11 +253,29 @@
         rank = lax.rem(tp + o, n_tp)
         send(part_out.at[o], part_in.at[tp], rs_send.at[o], rs_recv.at[tp], (inst, rank)).wait_send()
         give(o).wait_send()
-    for which in range(2):
-        for k in range(n_tp):
-            handoff(which, k).wait_send()
-            there = adopted_ref.at[0, 0, k, which]
-            send(there, there, kv_send.at[which, k], kv_recv.at[which, k], (other, k)).wait_recv()
+    for j in range(4 * n_tp):
+        handoff(j).wait_send()
+        phase, k = j // n_tp, j % n_tp
+        there = adopted_ref.at[0, 0, k, phase // 2, pl.ds(phase % 2 * half, half)]
+        send(there, there, kv_send.at[phase, k], kv_recv.at[phase, k], (other, k)).wait_recv()
+
+
+def place_outputs(mixed_ref, adopted_ref, mixed_out, adopted_out, sem):
+    count = adopted_ref.shape[2]
+    copies = [pltpu.make_async_copy(mixed_ref, mixed_out.at[0], sem.at[0])]
+    for row in range(count):
+        for which in range(2):
+            copies.append(
+                pltpu.make_async_copy(
+                    adopted_ref.at[0, 0, row, which],
+                    adopted_out.at[0, 0, row, which],
+                    sem.at[1 + 2 * row + which],
+                )
+            )
+    for copy in copies:
+        copy.start()
+    for copy in copies:
+        copy.wait()
 
 
 def on_device(n_inst, n_tp, source_cache, resident_cache, new_kv, queries, residual, lengths, out_weight):
@@ -299,8 +325,8 @@
             pltpu.VMEM((n_tp,) + stack, BF16),
             pltpu.VMEM(stack, F32),
             pltpu.VMEM((rows, model), BF16),
-            dma((2, n_tp)),
-            dma((2, n_tp)),
+            dma((4, n_tp)),
+            dma((4, n_tp)),
             dma((8,)),
             dma((adopt,)),
             dma((n_tp,)),
@@ -317,7 +343,19 @@
         ),
         name="handoff_attention",
     )(source_cache, resident_cache, new_kv, queries, residual, lengths, out_weight)
-    return (mixed[None], adopted)
+    return pl.pallas_call(
+        place_outputs,
+        out_shape=(
+            jax.ShapeDtypeStruct((1, rows, model), BF16),
+            jax.ShapeDtypeStruct(adopted.shape, BF16),
+        ),
+        in_specs=[any_spec, any_spec],
+        out_specs=(any_spec, any_spec),
+        scratch_shapes=[dma((1 + 2 * adopt,))],
+        compiler_params=pltpu.CompilerParams(vmem_limit_bytes=60 * 1024 * 1024),
+        cost_estimate=pl.CostEstimate(flops=0, bytes_accessed=4 * adopted.size, transcendentals=0),
+        name="place_outputs",
+    )(mixed, adopted)
 
 
 def solution(mesh):

time: 71.3 us -> 134 us (1.88)
  Pallas kernels: 65.8 us -> 133 us
  local copies, waits for them, and re-layouts: 4.71 us -> 0 us
    pallas_call x0 -> x1, Pallas kernels: none -> 72.7 us  [on_device(): pl.pallas_call(place_outputs, out_shape=(jax.ShapeDtypeStruct((1, rows, m...]
    pallas_call x1, Pallas kernels: 65.8 us -> 60.5 us  [on_device(): pl.pallas_call(functools.partial(kernel, dims), out_shape=(jax.ShapeDtype...]
    unnamed x2 -> x0, local copies, waits for them, and re-layouts: 4.71 us -> none
where the time goes in v3:
time: 134 us
  Pallas kernels  133 us (99%)
    pallas_call x1, Pallas kernels, on_device(): pl.pallas_call(place_outputs, out_shape=(jax.ShapeDtypeStruct((1, rows, m...  72.7 us
    pallas_call x1, Pallas kernels, on_device(): pl.pallas_call(functools.partial(kernel, dims), out_shape=(jax.ShapeDtype...  60.5 us

profile of v3, /device:TPU:0, one launch (start us, length us, event | category | flops | bytes accessed | tf_op | source)
XLA Modules:
  0.0 133.8 jit_solution(8229881515516564499)
XLA Ops:
  0.6 60.5 %handoff_attention.1 = (bf16[12,8192]{1,0:T(8,128)(2,1)}, bf16[1,1,4,2,512,256]{5,4,3,2,1,0:T(8,128)(2,1)}) custom-call(bf16[1,1,2,512,1024]{4,3,2,1,0:T(8,128)(2,1)} %source_ref.1, bf16[1,1,8,2,512,256]{5,4,3,2,1,0:T(8,128)(2,1)} %resident_ref.1, bf16[1,12,2,1024]{3,2,1,0:T(2,128)(2,1)} %newkv_ref.1, bf16[1,12,1024]{2,1,0:T(8,128)(2,1)} %query_ref.1, ...), custom_call_target="tpu_custom_call" | custom-call | flops 201326592 | bytes 16777216 | tf_op jit(solution)/shard_map/handoff_attention/pallas_call | solution.py:297
  61.2 72.7 %place_outputs.1 = (bf16[1,12,8192]{2,1,0:T(8,128)(2,1)}, bf16[1,1,4,2,512,256]{5,4,3,2,1,0:T(8,128)(2,1)}) custom-call(bf16[12,8192]{1,0:T(8,128)(2,1)} %get-tuple-element.4.mixed_ref, bf16[1,1,4,2,512,256]{5,4,3,2,1,0:T(8,128)(2,1)} %get-tuple-element.5.adopted_ref), custom_call_target="tpu_custom_call" | custom-call | bytes 4194304 | tf_op jit(solution)/shard_map/place_outputs/pallas_call | solution.py:346

commit v4 on v3

--- a/solution.py
+++ b/solution.py
@@ -25,10 +25,10 @@
     dims,
     source_ref, resident_ref, newkv_ref, query_ref, resid_ref, lens_ref, weight_ref,
     mixed_ref, adopted_ref,
-    source, resident, weight, q_raw, nk_raw, rs_raw, len_raw,
+    source, cache, resident, weight, q_raw, nk_raw, rs_raw, len_raw,
     qf, q_rows, q_in, nkf, nk_out, nk_in, resf, o_out, o_in, attn,
     part_out, part_in, final, total, mixed,
-    kv_send, kv_recv, load_sem, q_send, q_recv, nk_sem, o_send, o_recv,
+    kv_send, kv_recv, keep_sem, load_sem, q_send, q_recv, nk_sem, o_send, o_recv,
     rs_send, rs_recv, ag_send, ag_recv,
 ):
     n_inst, n_tp, adopt, res_rows, kv_dev, per_kv, span = dims
@@ -62,14 +62,14 @@
                 (query_ref, q_raw),
                 (newkv_ref, nk_raw),
                 (lens_ref, len_raw),
+                (source_ref, source),
                 (resident_ref, resident),
-                (source_ref, source),
                 (resid_ref, rs_raw),
                 (weight_ref, weight),
             )
         )
     ]
-    for load in loads[:3]:
+    for load in loads[:4]:
         load.start()
     pl.semaphore_wait(barrier, 2 * n_tp - 1)
 
@@ -84,14 +84,21 @@
         rank = lax.rem(tp + base + core * (n_tp // 2), n_tp)
         rows_of = pl.ds(piece * half, half)
         return pltpu.make_async_remote_copy(
-            src_ref=source_ref.at[0, 0, which, rows_of, my_columns(rank)],
-            dst_ref=adopted_ref.at[0, 0, tp, which, rows_of],
+            src_ref=source.at[0, 0, which, rows_of, my_columns(rank)],
+            dst_ref=cache.at[tp, which, rows_of],
             send_sem=kv_send.at[phase, k],
             recv_sem=kv_recv.at[phase, tp],
             device_id=(other, rank),
             device_id_type=MESH,
         )
 
+    def keep(j):
+        phase, k = j // n_tp, j % n_tp
+        which, rows_of = phase // 2, pl.ds(phase % 2 * half, half)
+        return pltpu.make_async_copy(
+            cache.at[k, which, rows_of], adopted_ref.at[0, 0, k, which, rows_of], keep_sem.at[phase, k]
+        )
+
     def start_handoff(first, last):
         for j in range(first * n_tp // 4, last * n_tp // 4):
             handoff(j).start()
@@ -102,8 +109,9 @@
             device_id=device, device_id_type=MESH,
         )
 
+    loads[3].wait()
     start_handoff(0, 2)
-    for load in loads[3:]:
+    for load in loads[4:]:
         load.start()
     for load in loads[:3]:
         load.wait()
@@ -171,11 +179,10 @@
             ),
         )
 
-    loads[3].wait()
+    loads[4].wait()
     for row in range(adopt, adopt + res_rows // 2):
         serve(row)
 
-    loads[4].wait()
     nk_send.wait_recv()
     for rank in range(n_tp):
         send(q_rows.at[rank], q_in.at[rank], q_send.at[rank], q_recv.at[rank], (other, rank)).wait_recv()
@@ -256,26 +263,30 @@
     for j in range(4 * n_tp):
         handoff(j).wait_send()
         phase, k = j // n_tp, j % n_tp
-        there = adopted_ref.at[0, 0, k, phase // 2, pl.ds(phase % 2 * half, half)]
+        rows_of = pl.ds(phase % 2 * half, half)
+        there = cache.at[k, phase // 2, rows_of]
         send(there, there, kv_send.at[phase, k], kv_recv.at[phase, k], (other, k)).wait_recv()
-
-
-def place_outputs(mixed_ref, adopted_ref, mixed_out, adopted_out, sem):
-    count = adopted_ref.shape[2]
-    copies = [pltpu.make_async_copy(mixed_ref, mixed_out.at[0], sem.at[0])]
-    for row in range(count):
+        keep(j).start()
+    for j in range(4 * n_tp):
+        keep(j).wait()
+
+
+def place_outputs(mixed_ref, adopted_ref, mixed_out, adopted_out, mixed, cache, load_sem, store_sem):
+    loads = [pltpu.make_async_copy(mixed_ref, mixed, load_sem.at[0])]
+    stores = [pltpu.make_async_copy(mixed, mixed_out.at[0], store_sem.at[0])]
+    for row in range(adopted_ref.shape[2]):
         for which in range(2):
-            copies.append(
-                pltpu.make_async_copy(
-                    adopted_ref.at[0, 0, row, which],
-                    adopted_out.at[0, 0, row, which],
-                    sem.at[1 + 2 * row + which],
-                )
-            )
-    for copy in copies:
-        copy.start()
-    for copy in copies:
-        copy.wait()
+            at = 1 + 2 * row + which
+            there = cache.at[row, which]
+            loads.append(pltpu.make_async_copy(adopted_ref.at[0, 0, row, which], there, load_sem.at[at]))
+            stores.append(pltpu.make_async_copy(there, adopted_out.at[0, 0, row, which], store_sem.at[at]))
+    for load in loads:
+        load.start()
+    for load, store in zip(loads, stores):
+        load.wait()
+        store.start()
+    for store in stores:
+        store.wait()
 
 
 def on_device(n_inst, n_tp, source_cache, resident_cache, new_kv, queries, residual, lengths, out_weight):
@@ -304,6 +315,7 @@
         out_specs=(any_spec, any_spec),
         scratch_shapes=[
             pltpu.VMEM(source_cache.shape, BF16),
+            pltpu.VMEM((adopt, 2, span, wide), BF16),
             pltpu.VMEM(resident_cache.shape, BF16),
             pltpu.VMEM(out_weight.shape, BF16),
             pltpu.VMEM(queries.shape, BF16),
@@ -325,6 +337,7 @@
             pltpu.VMEM((n_tp,) + stack, BF16),
             pltpu.VMEM(stack, F32),
             pltpu.VMEM((rows, model), BF16),
+            dma((4, n_tp)),
             dma((4, n_tp)),
             dma((4, n_tp)),
             dma((8,)),
@@ -351,7 +364,12 @@
         ),
         in_specs=[any_spec, any_spec],
         out_specs=(any_spec, any_spec),
-        scratch_shapes=[dma((1 + 2 * adopt,))],
+        scratch_shapes=[
+            pltpu.VMEM((rows, model), BF16),
+            pltpu.VMEM((adopt, 2, span, wide), BF16),
+            dma((1 + 2 * adopt,)),
+            dma((1 + 2 * adopt,)),
+        ],
         compiler_params=pltpu.CompilerParams(vmem_limit_bytes=60 * 1024 * 1024),
         cost_estimate=pl.CostEstimate(flops=0, bytes_accessed=4 * adopted.size, transcendentals=0),
         name="place_outputs",

time: 134 us -> 64.7 us (0.48)
  Pallas kernels: 133 us -> 63.9 us
    pallas_call x1, Pallas kernels: 72.7 us -> 2.5 us  [on_device(): pl.pallas_call(place_outputs, out_shape=(jax.ShapeDtypeStruct((1, rows, m...]
where the time goes in v4:
time: 64.7 us; the launch traced here: 64.6 us
  Pallas kernels  63.9 us (99%)
    pallas_call x1, Pallas kernels, on_device(): pl.pallas_call(functools.partial(kernel, dims), out_shape=(jax.ShapeDtype...  61.4 us
    pallas_call x1, Pallas kernels, on_device(): pl.pallas_call(place_outputs, out_shape=(jax.ShapeDtypeStruct((1, rows, m...  2.5 us

profile of v4, /device:TPU:0, one launch (start us, length us, event | category | flops | bytes accessed | tf_op | source)
XLA Modules:
  0.0 64.6 jit_solution(16185368386710080356)
XLA Ops:
  0.6 61.4 %handoff_attention.1 = (bf16[12,8192]{1,0:T(8,128)(2,1)}, bf16[1,1,4,2,512,256]{5,4,3,2,1,0:T(8,128)(2,1)}) custom-call(bf16[1,1,2,512,1024]{4,3,2,1,0:T(8,128)(2,1)} %source_ref.1, bf16[1,1,8,2,512,256]{5,4,3,2,1,0:T(8,128)(2,1)} %resident_ref.1, bf16[1,12,2,1024]{3,2,1,0:T(2,128)(2,1)} %newkv_ref.1, bf16[1,12,1024]{2,1,0:T(8,128)(2,1)} %query_ref.1, ...), custom_call_target="tpu_custom_call" | custom-call | flops 201326592 | bytes 16777216 | tf_op jit(solution)/shard_map/handoff_attention/pallas_call | solution.py:308
  62.1 2.5 %place_outputs.1 = (bf16[1,12,8192]{2,1,0:T(8,128)(2,1)}, bf16[1,1,4,2,512,256]{5,4,3,2,1,0:T(8,128)(2,1)}) custom-call(bf16[12,8192]{1,0:T(8,128)(2,1)} %get-tuple-element.4.mixed_ref, bf16[1,1,4,2,512,256]{5,4,3,2,1,0:T(8,128)(2,1)} %get-tuple-element.5.adopted_ref), custom_call_target="tpu_custom_call" | custom-call | bytes 4194304 | tf_op jit(solution)/shard_map/place_outputs/pallas_call | solution.py:359

commit v5 on v4

--- a/solution.py
+++ b/solution.py
@@ -27,9 +27,9 @@
     mixed_ref, adopted_ref,
     source, cache, resident, weight, q_raw, nk_raw, rs_raw, len_raw,
     qf, q_rows, q_in, nkf, nk_out, nk_in, resf, o_out, o_in, attn,
-    part_out, part_in, final, total, mixed,
+    part_out, part_in, final, total, half_out, half_in, mixed,
     kv_send, kv_recv, keep_sem, load_sem, q_send, q_recv, nk_sem, o_send, o_recv,
-    rs_send, rs_recv, ag_send, ag_recv,
+    rs_send, rs_recv, ag_send, ag_recv, cross_sem,
 ):
     n_inst, n_tp, adopt, res_rows, kv_dev, per_kv, span = dims
     rows = adopt + res_rows
@@ -40,7 +40,9 @@
     other = lax.rem(inst + n_inst // 2, n_inst)
     scale = 1.0 / math.sqrt(HD)
     model = weight_ref.shape[1]
-    share = model // n_tp
+    side = n_tp // 2
+    near, mine = tp // side * side, lax.rem(tp, side)
+    share = model // side
     pieces = pieces_of(rows)
     width = share // pieces
 
@@ -207,45 +209,57 @@
         place_row(row, o_in[row])
     loads[6].wait()
 
-    def project(rank, with_residual):
+    def project(part):
         a = attn[...].astype(BF16)
         parts = []
         for j in range(pieces):
-            at = pl.multiple_of(rank * share + j * width, HD)
-            value = jnp.dot(a, weight[:, pl.ds(at, width)], preferred_element_type=F32)
-            if with_residual:
-                value = value + resf[:, pl.ds(at, width)]
-            parts.append(value)
+            at = pl.multiple_of(part * share + j * width, HD)
+            parts.append(jnp.dot(a, weight[:, pl.ds(at, width)], preferred_element_type=F32))
         return jnp.concatenate(parts, axis=0)
 
-    @pl.loop(1, n_tp)
+    @pl.loop(1, side)
     def _(o):
-        rank = lax.rem(tp + o, n_tp)
-        part_out[o] = project(rank, False).astype(BF16)
-        send(part_out.at[o], part_in.at[tp], rs_send.at[o], rs_recv.at[tp], (inst, rank)).start()
+        part = lax.rem(mine + o, side)
+        part_out[o] = project(part).astype(BF16)
+        send(part_out.at[o], part_in.at[mine], rs_send.at[o], rs_recv.at[mine], (inst, near + part)).start()
 
     start_handoff(10, 12)
-    total[...] = project(tp, True)
-    for o in range(1, n_tp):
-        rank = lax.rem(tp + o, n_tp)
-        send(part_out.at[o], part_in.at[rank], rs_send.at[o], rs_recv.at[rank], (inst, rank)).wait_recv()
-        total[...] += part_in[rank].astype(F32)
-    final[tp] = total[...].astype(BF16)
+    total[...] = project(mine)
+    for o in range(1, side):
+        part = lax.rem(mine + o, side)
+        send(part_out.at[o], part_in.at[part], rs_send.at[o], rs_recv.at[part], (inst, near + part)).wait_recv()
+        total[...] += part_in[part].astype(F32)
+
+    half_out[...] = total[...].astype(BF16)
+    cross = send(
+        half_out, half_in, cross_sem.at[0], cross_sem.at[1], (inst, lax.rem(tp + side, n_tp))
+    )
+    cross.start()
+    start_handoff(12, 14)
+    cross.wait_recv()
+    extra = jnp.concatenate(
+        [
+            resf[:, pl.ds(pl.multiple_of(mine * share + j * width, HD), width)]
+            for j in range(pieces)
+        ],
+        axis=0,
+    )
+    final[mine] = (half_out[...].astype(F32) + half_in[...].astype(F32) + extra).astype(BF16)
 
     def give(o):
-        rank = lax.rem(tp + o, n_tp)
-        return send(final.at[tp], final.at[tp], ag_send.at[o], ag_recv.at[tp], (inst, rank))
-
-    for o in range(1, n_tp):
+        part = lax.rem(mine + o, side)
+        return send(final.at[mine], final.at[mine], ag_send.at[o], ag_recv.at[mine], (inst, near + part))
+
+    for o in range(1, side):
         give(o).start()
-    start_handoff(12, 16)
-    for o in range(1, n_tp):
-        rank = lax.rem(tp + o, n_tp)
-        send(final.at[rank], final.at[rank], ag_send.at[o], ag_recv.at[rank], (inst, rank)).wait_recv()
-    for rank in range(n_tp):
-        block = final[rank].astype(F32)
+    start_handoff(14, 16)
+    for o in range(1, side):
+        part = lax.rem(mine + o, side)
+        send(final.at[part], final.at[part], ag_send.at[o], ag_recv.at[part], (inst, near + part)).wait_recv()
+    for part in range(side):
+        block = final[part].astype(F32)
         for j in range(pieces):
-            at = rank * share + j * width
+            at = part * share + j * width
             mixed[:, at : at + width] = block[j * rows : (j + 1) * rows].astype(BF16)
     mixed_copy = pltpu.make_async_copy(mixed, mixed_ref, load_sem.at[7])
     mixed_copy.start()
@@ -256,9 +270,10 @@
     nk_send.wait_send()
     for copy in o_sends:
         copy.wait_send()
-    for o in range(1, n_tp):
-        rank = lax.rem(tp + o, n_tp)
-        send(part_out.at[o], part_in.at[tp], rs_send.at[o], rs_recv.at[tp], (inst, rank)).wait_send()
+    cross.wait_send()
+    for o in range(1, side):
+        part = lax.rem(mine + o, side)
+        send(part_out.at[o], part_in.at[mine], rs_send.at[o], rs_recv.at[mine], (inst, near + part)).wait_send()
         give(o).wait_send()
     for j in range(4 * n_tp):
         handoff(j).wait_send()
@@ -301,7 +316,8 @@
     wide = kv_dev * HD
     depth, model = out_weight.shape
     pieces = pieces_of(rows)
-    stack = (rows * pieces, model // n_tp // pieces)
+    side = n_tp // 2
+    stack = (rows * pieces, model // side // pieces)
     dims = (n_inst, n_tp, adopt, res_rows, kv_dev, per_kv, span)
     dma = pltpu.SemaphoreType.DMA
     any_spec = pl.BlockSpec(memory_space=pl.ANY)
@@ -332,10 +348,12 @@
             pltpu.VMEM((n_tp, per_dev, HD), F32),
             pltpu.VMEM((adopt, per_dev, HD), F32),
             pltpu.VMEM((rows, depth), F32),
-            pltpu.VMEM((n_tp,) + stack, BF16),
-            pltpu.VMEM((n_tp,) + stack, BF16),
-            pltpu.VMEM((n_tp,) + stack, BF16),
+            pltpu.VMEM((side,) + stack, BF16),
+            pltpu.VMEM((side,) + stack, BF16),
+            pltpu.VMEM((side,) + stack, BF16),
             pltpu.VMEM(stack, F32),
+            pltpu.VMEM(stack, BF16),
+            pltpu.VMEM(stack, BF16),
             pltpu.VMEM((rows, model), BF16),
             dma((4, n_tp)),
             dma((4, n_tp)),
@@ -347,7 +365,8 @@
             dma((n_tp,)),
             dma((adopt,)),
         ]
-        + [dma((n_tp,))] * 4,
+        + [dma((side,))] * 4
+        + [dma((2,))],
         compiler_params=pltpu.CompilerParams(
             collective_id=0, has_side_effects=True, vmem_limit_bytes=60 * 1024 * 1024
         ),

time: 64.7 us -> 62.9 us (0.972)
  Pallas kernels: 63.9 us -> 62.1 us
    pallas_call x1, Pallas kernels: 61.4 us -> 59.6 us  [on_device(): pl.pallas_call(functools.partial(kernel, dims), out_shape=(jax.ShapeDtype...]
where the time goes in v5:
time: 62.9 us; the launch traced here: 62.7 us
  Pallas kernels  62.1 us (99%)
  between operations  0.64 us (1%)
    pallas_call x1, Pallas kernels, on_device(): pl.pallas_call(functools.partial(kernel, dims), out_shape=(jax.ShapeDtype...  59.6 us
    pallas_call x1, Pallas kernels, on_device(): pl.pallas_call(place_outputs, out_shape=(jax.ShapeDtypeStruct((1, rows, m...  2.5 us

profile of v5, /device:TPU:0, one launch (start us, length us, event | category | flops | bytes accessed | tf_op | source)
XLA Modules:
  0.0 62.7 jit_solution(8815032640164832502)
XLA Ops:
  0.6 59.6 %handoff_attention.1 = (bf16[12,8192]{1,0:T(8,128)(2,1)}, bf16[1,1,4,2,512,256]{5,4,3,2,1,0:T(8,128)(2,1)}) custom-call(bf16[1,1,2,512,1024]{4,3,2,1,0:T(8,128)(2,1)} %source_ref.1, bf16[1,1,8,2,512,256]{5,4,3,2,1,0:T(8,128)(2,1)} %resident_ref.1, bf16[1,12,2,1024]{3,2,1,0:T(2,128)(2,1)} %newkv_ref.1, bf16[1,12,1024]{2,1,0:T(8,128)(2,1)} %query_ref.1, ...), custom_call_target="tpu_custom_call" | custom-call | flops 201326592 | bytes 16777216 | tf_op jit(solution)/shard_map/handoff_attention/pallas_call | solution.py:324
  60.2 2.5 %place_outputs.1 = (bf16[1,12,8192]{2,1,0:T(8,128)(2,1)}, bf16[1,1,4,2,512,256]{5,4,3,2,1,0:T(8,128)(2,1)}) custom-call(bf16[12,8192]{1,0:T(8,128)(2,1)} %get-tuple-element.4.mixed_ref, bf16[1,1,4,2,512,256]{5,4,3,2,1,0:T(8,128)(2,1)} %get-tuple-element.5.adopted_ref), custom_call_target="tpu_custom_call" | custom-call | bytes 4194304 | tf_op jit(solution)/shard_map/place_outputs/pallas_call | solution.py:378

commit v6 on v5

--- a/solution.py
+++ b/solution.py
@@ -198,7 +198,7 @@
         copy = send(o_out.at[rank], o_in.at[tp], o_send.at[rank], o_recv.at[tp], (other, rank))
         copy.start()
         o_sends.append(copy)
-    start_handoff(6, 10)
+    start_handoff(6, 11)
 
     for row in range(adopt + res_rows // 2, rows):
         serve(row)
@@ -223,7 +223,7 @@
         part_out[o] = project(part).astype(BF16)
         send(part_out.at[o], part_in.at[mine], rs_send.at[o], rs_recv.at[mine], (inst, near + part)).start()
 
-    start_handoff(10, 12)
+    start_handoff(11, 14)
     total[...] = project(mine)
     for o in range(1, side):
         part = lax.rem(mine + o, side)
@@ -235,7 +235,7 @@
         half_out, half_in, cross_sem.at[0], cross_sem.at[1], (inst, lax.rem(tp + side, n_tp))
     )
     cross.start()
-    start_handoff(12, 14)
+    start_handoff(14, 16)
     cross.wait_recv()
     extra = jnp.concatenate(
         [
@@ -252,7 +252,6 @@
 
     for o in range(1, side):
         give(o).start()
-    start_handoff(14, 16)
     for o in range(1, side):
         part = lax.rem(mine + o, side)
         send(final.at[part], final.at[part], ag_send.at[o], ag_recv.at[part], (inst, near + part)).wait_recv()

time: 62.9 us -> 64 us (1.017)
  Pallas kernels: 62.1 us -> 62.8 us
    pallas_call x1, Pallas kernels: 59.6 us -> 60.3 us  [on_device(): pl.pallas_call(functools.partial(kernel, dims), out_shape=(jax.ShapeDtype...]
where the time goes in v6:
time: 64 us; the launch traced here: 63.5 us
  Pallas kernels  62.8 us (98%)
  between operations  0.64 us (1%)
    pallas_call x1, Pallas kernels, on_device(): pl.pallas_call(functools.partial(kernel, dims), out_shape=(jax.ShapeDtype...  60.3 us
    pallas_call x1, Pallas kernels, on_device(): pl.pallas_call(place_outputs, out_shape=(jax.ShapeDtypeStruct((1, rows, m...  2.5 us

profile of v6, /device:TPU:0, one launch (start us, length us, event | category | flops | bytes accessed | tf_op | source)
XLA Modules:
  0.0 63.5 jit_solution(4627923566909137680)
XLA Ops:
  0.6 60.3 %handoff_attention.1 = (bf16[12,8192]{1,0:T(8,128)(2,1)}, bf16[1,1,4,2,512,256]{5,4,3,2,1,0:T(8,128)(2,1)}) custom-call(bf16[1,1,2,512,1024]{4,3,2,1,0:T(8,128)(2,1)} %source_ref.1, bf16[1,1,8,2,512,256]{5,4,3,2,1,0:T(8,128)(2,1)} %resident_ref.1, bf16[1,12,2,1024]{3,2,1,0:T(2,128)(2,1)} %newkv_ref.1, bf16[1,12,1024]{2,1,0:T(8,128)(2,1)} %query_ref.1, ...), custom_call_target="tpu_custom_call" | custom-call | flops 201326592 | bytes 16777216 | tf_op jit(solution)/shard_map/handoff_attention/pallas_call | solution.py:323
  61.0 2.5 %place_outputs.1 = (bf16[1,12,8192]{2,1,0:T(8,128)(2,1)}, bf16[1,1,4,2,512,256]{5,4,3,2,1,0:T(8,128)(2,1)}) custom-call(bf16[12,8192]{1,0:T(8,128)(2,1)} %get-tuple-element.4.mixed_ref, bf16[1,1,4,2,512,256]{5,4,3,2,1,0:T(8,128)(2,1)} %get-tuple-element.5.adopted_ref), custom_call_target="tpu_custom_call" | custom-call | bytes 4194304 | tf_op jit(solution)/shard_map/place_outputs/pallas_call | solution.py:377

commit v7 on v5

--- a/solution.py
+++ b/solution.py
@@ -73,6 +73,18 @@
     ]
     for load in loads[:4]:
         load.start()
+    for load in loads[:3]:
+        load.wait()
+
+    def rows_to_heads(first, last):
+        for row in range(first, last):
+            q_rows[row] = jnp.concatenate(
+                [qf[row : row + 1, h * HD : (h + 1) * HD] for h in range(per_dev)], axis=0
+            )
+
+    qf[...] = q_raw[0].astype(F32)
+    nk_out[...] = nk_raw[0, tp].astype(F32)
+    rows_to_heads(0, adopt)
     pl.semaphore_wait(barrier, 2 * n_tp - 1)
 
     core = lax.rem(inst, 2)
@@ -111,22 +123,6 @@
             device_id=device, device_id_type=MESH,
         )
 
-    loads[3].wait()
-    start_handoff(0, 2)
-    for load in loads[4:]:
-        load.start()
-    for load in loads[:3]:
-        load.wait()
-
-    def rows_to_heads(first, last):
-        for row in range(first, last):
-            q_rows[row] = jnp.concatenate(
-                [qf[row : row + 1, h * HD : (h + 1) * HD] for h in range(per_dev)], axis=0
-            )
-
-    qf[...] = q_raw[0].astype(F32)
-    nk_out[...] = nk_raw[0, tp].astype(F32)
-    rows_to_heads(0, adopt)
     q_sends = [
         send(q_rows.at[r], q_in.at[tp], q_send.at[r], q_recv.at[tp], (other, r)) for r in range(adopt)
     ]
@@ -134,7 +130,10 @@
     for copy in q_sends:
         copy.start()
     nk_send.start()
-    start_handoff(2, 6)
+    loads[3].wait()
+    start_handoff(0, 4)
+    for load in loads[4:]:
+        load.start()
     rows_to_heads(adopt, rows)
     nkf[...] = nk_raw[0, :, :, my_columns(tp)].astype(F32)
 
@@ -198,7 +197,7 @@
         copy = send(o_out.at[rank], o_in.at[tp], o_send.at[rank], o_recv.at[tp], (other, rank))
         copy.start()
         o_sends.append(copy)
-    start_handoff(6, 10)
+    start_handoff(4, 9)
 
     for row in range(adopt + res_rows // 2, rows):
         serve(row)
@@ -223,7 +222,7 @@
         part_out[o] = project(part).astype(BF16)
         send(part_out.at[o], part_in.at[mine], rs_send.at[o], rs_recv.at[mine], (inst, near + part)).start()
 
-    start_handoff(10, 12)
+    start_handoff(9, 12)
     total[...] = project(mine)
     for o in range(1, side):
         part = lax.rem(mine + o, side)

time: 62.9 us -> 66.7 us (1.060)
  Pallas kernels: 62.1 us -> 65.9 us
    pallas_call x1, Pallas kernels: 59.6 us -> 63.4 us  [on_device(): pl.pallas_call(functools.partial(kernel, dims), out_shape=(jax.ShapeDtype...]
where the time goes in v7:
time: 66.7 us; the launch traced here: 66.5 us
  Pallas kernels  65.9 us (99%)
    pallas_call x1, Pallas kernels, on_device(): pl.pallas_call(functools.partial(kernel, dims), out_shape=(jax.ShapeDtype...  63.4 us
    pallas_call x1, Pallas kernels, on_device(): pl.pallas_call(place_outputs, out_shape=(jax.ShapeDtypeStruct((1, rows, m...  2.5 us

profile of v7, /device:TPU:0, one launch (start us, length us, event | category | flops | bytes accessed | tf_op | source)
XLA Modules:
  0.0 66.5 jit_solution(18022813868720775199)
XLA Ops:
  0.6 63.4 %handoff_attention.1 = (bf16[12,8192]{1,0:T(8,128)(2,1)}, bf16[1,1,4,2,512,256]{5,4,3,2,1,0:T(8,128)(2,1)}) custom-call(bf16[1,1,2,512,1024]{4,3,2,1,0:T(8,128)(2,1)} %source_ref.1, bf16[1,1,8,2,512,256]{5,4,3,2,1,0:T(8,128)(2,1)} %resident_ref.1, bf16[1,12,2,1024]{3,2,1,0:T(2,128)(2,1)} %newkv_ref.1, bf16[1,12,1024]{2,1,0:T(8,128)(2,1)} %query_ref.1, ...), custom_call_target="tpu_custom_call" | custom-call | flops 201326592 | bytes 16777216 | tf_op jit(solution)/shard_map/handoff_attention/pallas_call | solution.py:323
  64.0 2.5 %place_outputs.1 = (bf16[1,12,8192]{2,1,0:T(8,128)(2,1)}, bf16[1,1,4,2,512,256]{5,4,3,2,1,0:T(8,128)(2,1)}) custom-call(bf16[12,8192]{1,0:T(8,128)(2,1)} %get-tuple-element.4.mixed_ref, bf16[1,1,4,2,512,256]{5,4,3,2,1,0:T(8,128)(2,1)} %get-tuple-element.5.adopted_ref), custom_call_target="tpu_custom_call" | custom-call | bytes 4194304 | tf_op jit(solution)/shard_map/place_outputs/pallas_call | solution.py:377
